TPU v7x, 256 devices: a whole 4x4x8 slice. The times are simulated.
256 devices in a mesh: tm: 16 (over y_lo, x, core), space: 16 (over z, y_hi).
Axes of the slice: x: 4, y: 4 (y_hi: 2, y_lo: 2; y = y_hi * 2 + y_lo), z: 8, core: 2. Of those that a mesh axis runs over, the one named last changes fastest.
Arguments:
- sources: float32 [192, 64, 32, 128], P('tm', None, 'space'), may hold values from -6 to 6
- fine_volume: float32 [64, 64], replicated
- fine_faces: float32 [6, 2, 64, 64], replicated
- coarse_volume: float32 [64, 64], replicated
- coarse_faces: float32 [6, 2, 64, 64], replicated
- flow_kinds: int32 [6, 32, 128], P(None, 'space'), may hold values from 0 to 1
- neighbours: int32 [4, 128], replicated, may hold values from 0 to 127, as said below
Outputs:
- iterate: float32 [192, 64, 32, 128], P('tm', None, 'space')
Inputs may be any that keep to these rules, and one draw needn't show every extreme that they name: `neighbours`: row f lists, for each element, the element beside it across side face f of a periodic 8 x 16 grid of elements whose labels are shuffled; rows 0 and 1 are opposite faces, as are rows 2 and 3, and each row names every element once.
All inputs are finite; a program needn't handle non-finite values.
Results may differ from a plain program's by a relative error of at most 0.0001.
Values sent between devices are 32-bit elements; how exact they have to be, the bound alone decides.
A program may use at most 64 MiB of HBM per device.

v0:
```python
import jax
import jax.numpy as jnp
from jax import lax
from jax.sharding import PartitionSpec as P

CF = 4


highest = lax.Precision.HIGHEST


def with_halo(block, sides, width):
    for axis, dim in sides:
        count = lax.axis_size(axis)
        forward = [(i, i + 1) for i in range(count - 1)]
        backward = [(target, source) for source, target in forward]
        low = lax.ppermute(
            lax.slice_in_dim(block, block.shape[dim] - width, None, axis=dim), axis, forward
        )
        high = lax.ppermute(lax.slice_in_dim(block, 0, width, axis=dim), axis, backward)
        block = jnp.concatenate([low, block, high], axis=dim)
    return block


def from_behind(value, axis, steps):
    count = lax.axis_size(axis)
    leading, last = (max(0, -steps), min(count, count - steps))
    return lax.ppermute(value, axis, [(source, source + steps) for source in range(leading, last)])


def advance(field, volume, faces_op, flow_kinds, neighbours):
    result = jnp.einsum("ab,jbzp->jazp", volume, field, precision=highest)
    for face_id in range(4):
        pair_prod = jnp.einsum("kab,jbzp->kjazp", faces_op[face_id], field, precision=highest)
        shifted = jnp.take(pair_prod, neighbours[face_id], axis=4)
        result = result + jnp.where(flow_kinds[face_id] == 1, shifted[1], shifted[0])
    padded = with_halo(field, (("space", 2),), 1)
    layer_count = field.shape[2]
    for face_id, offset in ((4, 0), (5, 2)):
        pair_prod = jnp.einsum(
            "kab,jbzp->kjazp",
            faces_op[face_id],
            padded[:, :, offset : offset + layer_count],
            precision=highest,
        )
        result = result + jnp.where(flow_kinds[face_id] == 1, pair_prod[1], pair_prod[0])
    return result


def on_device(
    sources, fine_volume, fine_faces, coarse_volume, coarse_faces, flow_kinds, neighbours
):
    tail = sources.shape[1:]
    blocks = sources.shape[0] // CF
    forcing = sources.reshape((blocks, CF) + tail)

    def fine_step(field):
        return advance(field, fine_volume, fine_faces, flow_kinds, neighbours)

    def coarse_step(state):
        return advance(state[None], coarse_volume, coarse_faces, flow_kinds, neighbours)[0]

    def relax(c_states):
        current = c_states
        states = [current]
        for inner in range(1, CF):
            current = fine_step(current) + forcing[:, inner]
            states.append(current)
        return jnp.stack(states, 1)

    c_states = jnp.zeros((blocks,) + tail, jnp.float32)
    fine_all = relax(c_states)
    incoming = from_behind(fine_all[blocks - 1, CF - 1], "tm", 1)
    before = jnp.concatenate([incoming[None], fine_all[: blocks - 1, CF - 1]], 0)
    c_states = fine_step(before) + forcing[:, 0]
    fine_all = relax(c_states)
    incoming = from_behind(fine_all[blocks - 1, CF - 1], "tm", 1)
    before = jnp.concatenate([incoming[None], fine_all[: blocks - 1, CF - 1]], 0)
    residue = fine_step(before) + forcing[:, 0] - c_states

    def sweep(entering):
        current = entering
        collected = []
        for interval in range(blocks):
            current = coarse_step(current) + residue[interval]
            collected.append(current)
        return (current, jnp.stack(collected, 0))

    def segment(counter, carry):
        last_state, previous = carry
        entering = from_behind(last_state, "tm", 1)
        return sweep(entering)

    start = (jnp.zeros(tail, jnp.float32), jnp.zeros((blocks,) + tail, jnp.float32))
    final_state, correction = lax.fori_loop(0, lax.axis_size("tm"), segment, start)
    fine_all = relax(c_states + correction)
    return fine_all.reshape(sources.shape)


def solution(mesh):
    in_specs = (P("tm", None, "space", None), P(), P(), P(), P(), P(None, "space", None), P())
    out_specs = P("tm", None, "space", None)
    return jax.shard_map(
        on_device, mesh=mesh, in_specs=in_specs, out_specs=out_specs, check_vma=False
    )
```

profile of v0, /device:TPU:8, one launch (start us, length us, event | category | flops | bytes accessed | tf_op | source)
XLA Modules:
  0.0 1377.2 jit_solution(11620997076344729594)
XLA Ops:
  1.4 6.1 collective-permute-start.7
  70.7 6.1 collective-permute-start.11
  79.4 5.5 collective-permute-done.12
  87.9 5.7 collective-permute-done.13
  185.8 5.5 collective-permute-done.19
  217.9 5.5 collective-permute-done.21
  226.4 5.7 collective-permute-done.22
  256.9 6.0 collective-permute-start.23
  265.6 5.6 collective-permute-done.24
  272.7 1003.4 %while.13 = (s32[]{:T(128)}, f32[64,2,128]{2,0,1:T(8,128)S(1)}, f32[3,64,2,128]{3,1,2,0:T(8,128)}, f32[64,64]{1,0:T(8,128)S(1)}, s32[6,2,128]{2,1,0:T(2,128)S(1)...) while((s32[]{:T(128)}, f32[64,2,128]{2,0,1:T(8,128)S(1)}, ...), condition=%wide.region_1.4_spmd.clone, body=%wide.region_0.3_spmd.sunk.clone | while | flops 491971072 | bytes 22374764 | solution.py:95
  275.1 5.7 collective-permute-done
  286.9 6.3 collective-permute-start.2
  307.2 6.3 collective-permute-start.4
  315.3 5.5 collective-permute-done.3
  342.0 5.7 collective-permute-done
  404.4 5.7 collective-permute-done
  440.8 5.5 collective-permute-done.3
  467.5 5.7 collective-permute-done
  529.7 6.0 collective-permute-done
  592.1 5.7 collective-permute-done
  654.6 5.7 collective-permute-done
  716.7 5.7 collective-permute-done
  779.0 5.7 collective-permute-done
  841.3 5.7 collective-permute-done
  903.6 6.0 collective-permute-done
  966.4 5.7 collective-permute-done
  1028.6 6.0 collective-permute-done
  1091.0 5.7 collective-permute-done
  1153.5 5.7 collective-permute-done
  1215.6 5.7 collective-permute-done
  1302.2 5.5 collective-permute-done.26
  1334.2 5.6 collective-permute-done.28
  (1896 shorter events, 1187.9 us)
Async XLA Ops:
  0.0 23.9 %collective-permute-start.8 = (f32[3,64,1,128]{3,1,2,0:T(8,128)S(1)}, f32[3,64,1,128]{3,1,2,0:T(8,128)S(1)}, u32[]{:S(2)}, u32[]{:S(2)}) collective-permute-start(f32[3,64,1,128]{3,1,2,0:T(8,128)S(1)} %broadcast.198), channel_id=1, source_target_pairs={{1,0},{2,1},{3,2},{4,3},{5,4},{6,5},{7,6},{8,7},{9,8},{10,9},{11,1... | collective-permute-start | bytes 294920 | tf_op jit(solution)/shard_map/ppermute | solution.py:20
  1.4 22.9 %collective-permute-start.7 = (f32[3,64,1,128]{3,1,2,0:T(8,128)S(1)}, f32[3,64,1,128]{3,1,2,0:T(8,128)S(1)}, u32[]{:S(2)}, u32[]{:S(2)}) collective-permute-start(f32[3,64,1,128]{3,1,2,0:T(8,128)S(1)} %broadcast.198), channel_id=1, source_target_pairs={{0,1},{1,2},{2,3},{3,4},{4,5},{5,6},{6,7},{7,8},{8,9},{9,10},{10,1... | collective-permute-start | bytes 294920 | tf_op jit(solution)/shard_map/ppermute | solution.py:17
  29.2 21.0 %collective-permute-start.9 = (f32[3,64,1,128]{3,1,2,0:T(8,128)S(1)}, f32[3,64,1,128]{3,1,2,0:T(8,128)S(1)}, u32[]{:S(2)}, u32[]{:S(2)}) collective-permute-start(f32[3,64,1,128]{3,1,2,0:T(8,128)S(1)} %get-tuple-element.121), channel_id=1, source_target_pairs={{0,1},{1,2},{2,3},{3,4},{4,5},{5,6},{6,7},{7,8},{8,9},{9,10},{10,1... | collective-permute-start | bytes 294920 | tf_op jit(solution)/shard_map/ppermute | solution.py:17
  34.4 16.3 %collective-permute-start.10 = (f32[3,64,1,128]{3,1,2,0:T(8,128)S(1)}, f32[3,64,1,128]{3,1,2,0:T(8,128)S(1)}, u32[]{:S(2)}, u32[]{:S(2)}) collective-permute-start(f32[3,64,1,128]{3,1,2,0:T(8,128)S(1)} %get-tuple-element.122), channel_id=1, source_target_pairs={{1,0},{2,1},{3,2},{4,3},{5,4},{6,5},{7,6},{8,7},{9,8},{10,9},{11,1... | collective-permute-start | bytes 294920 | tf_op jit(solution)/shard_map/ppermute | solution.py:20
  70.7 8.3 collective-permute-start.11
  76.8 8.1 collective-permute-start.12
  85.9 7.7 collective-permute-start.13
  112.3 8.6 collective-permute-start.14
  117.7 8.1 collective-permute-start.15
  149.7 8.1 collective-permute-start.17
  183.2 8.1 collective-permute-start.19
  215.3 8.1 collective-permute-start.21
  224.5 7.7 collective-permute-start.22
  256.9 8.2 collective-permute-start.23
  263.0 8.1 collective-permute-start.24
  273.0 7.7 collective-permute-start
  286.9 7.9 collective-permute-start.2
  307.2 7.9 collective-permute-start.4
  339.9 7.7 collective-permute-start
  402.4 7.7 collective-permute-start
  465.5 7.7 collective-permute-start
  527.7 8.0 collective-permute-start
  590.1 7.7 collective-permute-start
  652.6 7.7 collective-permute-start
  714.7 7.7 collective-permute-start
  777.0 7.8 collective-permute-start
  839.3 7.7 collective-permute-start
  901.6 8.0 collective-permute-start
  1026.6 8.0 collective-permute-start
  1299.6 8.1 collective-permute-start.26
  1331.6 8.1 collective-permute-start.28
  1366.1 8.1 collective-permute-start.30
  (176 other events, 1932.4 us)
where the time goes:
time: 1390 us; the launch traced here: 1380 us
  waiting for transfers between devices  433 us (31%)
  local copies, waits for them, and re-layouts  391 us (28%)
  starting transfers between devices  365 us (26%)
  matrix products  141 us (10%)
  other arithmetic  36.7 us (3%)
    gather x472, local copies, waits for them, and re-layouts, advance(): shifted = jnp.take(pair_prod, neighbours[face_id], axis=4)  318 us
    ppermute x59, waiting for transfers between devices, with_halo(): lax.ppermute(lax.slice_in_dim(block, 0, width, axis=dim), axis, backward)  311 us
    ppermute x59, starting transfers between devices, with_halo(): lax.ppermute(lax.slice_in_dim(block, block.shape[dim] - width, None, axis...  252 us
    ppermute x18, waiting for transfers between devices, from_behind(): lax.ppermute(value, axis, [(source, source + steps) for source in range(l...  103 us
    dot_general x236, matrix products, advance(): jnp.einsum('kab,jbzp->kjazp', faces_op[face_id], field, precision=highest)  90.8 us
    ppermute x59, starting transfers between devices, with_halo(): lax.ppermute(lax.slice_in_dim(block, 0, width, axis=dim), axis, backward)  77.8 us
    dot_general x118, matrix products, advance(): jnp.einsum('kab,jbzp->kjazp', faces_op[face_id], padded[:, :, offset:offs...  34.4 us
    ppermute x18, starting transfers between devices, from_behind(): lax.ppermute(value, axis, [(source, source + steps) for source in range(l...  34.4 us
  transfers between devices with their start and end apart: 136, of which 132 were waited for; matrix products, arithmetic and copies ran while one was open for 3% of the time, Pallas kernels for 0%

commit v1 on v0

v1 whole, which is shorter than its diff:
```python
import jax
import jax.numpy as jnp
from jax import lax
from jax.experimental import pallas as pl
from jax.experimental.pallas import tpu as pltpu
from jax.sharding import PartitionSpec as P

CF = 4
NODES = 64
PLANE = 128
OWN = 2
KH = 4
MESH = pl.DeviceIdType.MESH
f32, bf16 = jnp.float32, jnp.bfloat16


def dot(a, b):
    return jnp.dot(a, b, preferred_element_type=f32)


def split(value):
    high = value.astype(bf16)
    low = (value - high.astype(f32)).astype(bf16)
    return high, low


def span(halo, d):
    low = halo - OWN * d
    first, last = max(low, 0), min(low + OWN, OWN + 2 * halo)
    return first, last - first, first - low


def kernel(sections, positions, layers, intervals,
           x_ref, fv_ref, ff_ref, cv_ref, cf_ref, kinds_ref, nb_ref, out_ref,
           fine_op, coarse_op, kwin, idx, w0, w1, w2, w3, aout, ain, ww, rw0, rw1, r2, lout, ein, eout,
           send_sem, recv_sem):
    tm, sp = lax.axis_index("tm"), lax.axis_index("space")

    def at(d, ahead):
        return (lax.rem(tm + ahead + sections, sections), lax.rem(sp + d + positions, positions))

    partners = [at(d, 0) for d in (-3, -2, -1, 1, 2, 3)]
    partners += [at(d, a) for a in (-1, 1) for d in range(-3, 4)]
    barrier = pltpu.get_barrier_semaphore()
    for device in partners:
        pl.semaphore_signal(barrier, inc=1, device_id=device, device_id_type=MESH)

    def source(t):
        return [x_ref[pl.ds(t * OWN * NODES + o, NODES, stride=OWN), :] for o in range(OWN)]

    for i in range(intervals):
        for win, halo, inner in ((w1, 3, 1), (w2, 2, 2), (w3, 1, 3)):
            for o, value in enumerate(source(i * CF + inner)):
                win[i, halo + o] = value
    for o, value in enumerate(source(0)):
        w0[4 + o] = value
    for f in range(4):
        idx[f] = jnp.broadcast_to(nb_ref[f : f + 1, :], (8, PLANE))
    opposite = (1, 0, 3, 2)
    for o in range(OWN):
        for f in range(6):
            row = kinds_ref[f, o : o + 1, :].astype(f32)
            if f < 4:
                wide = jnp.broadcast_to(row, (8, PLANE))
                row = jnp.take_along_axis(wide, idx[opposite[f]], axis=1, mode="promise_in_bounds")[0:1]
            kwin[KH + o, f : f + 1, :] = row
        kwin[KH + o, 6:8, :] = jnp.zeros((2, PLANE), f32)

    count = [0]

    def copy(src, dst, d, ahead):
        k = count[0]
        count[0] += 1
        return pltpu.make_async_remote_copy(
            src_ref=src, dst_ref=dst, send_sem=send_sem.at[k], recv_sem=recv_sem.at[k],
            device_id=at(d, ahead), device_id_type=MESH)

    def swap(win, halo, reach, lead=None):
        made = []
        for d in [s * r for r in range(1, reach + 1) for s in (1, -1)]:
            first, size, skip = span(halo, d)
            src, dst = pl.ds(halo + skip, size), pl.ds(first, size)
            if lead is None:
                made.append(copy(win.at[src], win.at[dst], d, 0))
            else:
                made.append(copy(win.at[lead, src], win.at[lead, dst], d, 0))
        return made

    def hop(block, win, halo, reach):
        made = []
        for d in [0] + [s * r for r in range(1, reach + 1) for s in (1, -1)]:
            first, size, skip = span(halo, d)
            made.append(copy(block.at[pl.ds(skip, size)], win.at[pl.ds(first, size)], d, 1))
        return made

    def start(copies):
        for c in copies:
            c.start()

    def received(copies):
        for c in copies:
            c.wait_recv()

    every = pl.ds(0, intervals)
    swap1 = swap(w1, 3, 2, every)
    swapk = swap(kwin, KH, 2)
    swap2 = swap(w2, 2, 1, every)
    swap3 = swap(w3, 1, 1, every)
    swap0 = swap(w0, 4, 2)
    first_copies = swap1 + swapk + swap2 + swap3 + swap0
    pl.semaphore_wait(barrier, len(partners))
    start(first_copies)

    rows = lax.broadcasted_iota(jnp.int32, (NODES, 2 * NODES), 0)
    cols = lax.broadcasted_iota(jnp.int32, (NODES, 2 * NODES), 1)
    twice = (rows == lax.rem(cols, NODES)).astype(bf16)

    def build(op, volume, faces):
        blocks = [volume[...]] + [faces[f, k] for f in range(6) for k in range(2)]
        for n, block in enumerate(blocks):
            for part, value in enumerate(split(block)):
                op[n * NODES : (n + 1) * NODES, part * 128 : (part + 1) * 128] = dot(value, twice).astype(bf16)

    build(fine_op, fv_ref, ff_ref)
    build(coarse_op, cv_ref, cf_ref)
    index = [jnp.broadcast_to(idx[f, 0:1, :], (NODES, PLANE)) for f in range(4)]

    def inside(z):
        return jnp.logical_and(z >= 0, z < layers)

    def clean(values):
        halo = (len(values) - OWN) // 2
        return [
            v if halo <= l < halo + OWN else jnp.where(inside(sp * OWN - halo + l), v, 0.0)
            for l, v in enumerate(values)
        ]

    def advance(groups, op):
        n = len(groups[0]) - 2
        halo = (n - OWN) // 2
        parts = []
        for values in groups:
            both = [split(v) for v in clean(values)]
            parts.append([jnp.concatenate([h, w, h, w], 0) for h, w in both])
        centre = dot(op[...], jnp.concatenate([v for g in parts for v in g[1:-1]], 1))
        below = dot(op[576:704, :], jnp.concatenate([g[0] for g in parts], 1))
        above = dot(op[704:832, :], jnp.concatenate([g[-1] for g in parts], 1))
        results = []
        for g in range(len(groups)):
            result = []
            for l in range(n):
                def block(b, at_layer=l):
                    c = (g * n + at_layer) * PLANE
                    return centre[b * NODES : (b + 1) * NODES, c : c + PLANE]

                def kind(f):
                    row = kwin[KH - halo + l, f : f + 1, :]
                    return jnp.broadcast_to(row, (NODES, PLANE)) > 0.5

                total = block(0)
                for f in range(4):
                    chosen = jnp.where(kind(f), block(2 + 2 * f), block(1 + 2 * f))
                    total = total + jnp.take_along_axis(chosen, index[f], axis=1, mode="promise_in_bounds")
                here = slice(g * PLANE, (g + 1) * PLANE)
                if l > 0:
                    low = block(9, l - 1), block(10, l - 1)
                else:
                    low = below[:NODES, here], below[NODES:, here]
                if l < n - 1:
                    high = block(11, l + 1), block(12, l + 1)
                else:
                    high = above[:NODES, here], above[NODES:, here]
                total = total + jnp.where(kind(4), low[1], low[0])
                total = total + jnp.where(kind(5), high[1], high[0])
                result.append(total)
            results.append(result)
        return results

    def read(win, halo, keep, i=None):
        rows = range(halo - keep, halo + OWN + keep)
        return [win[r] if i is None else win[i, r] for r in rows]

    def plus(groups, others):
        return [[a + b for a, b in zip(g, h)] for g, h in zip(groups, others)]

    def all_of(win, halo, keep):
        return [read(win, halo, keep, i) for i in range(intervals)]

    received(swap1 + swapk)
    state = advance(all_of(w1, 3, 3), fine_op)
    received(swap2)
    state = plus(state, all_of(w2, 2, 2))
    state = advance(state, fine_op)
    received(swap3)
    state = plus(state, all_of(w3, 1, 1))
    state = advance(state, fine_op)
    for o in range(OWN):
        aout[o] = state[intervals - 1][o]
    hop_a = hop(aout, ain, 4, 2)
    start(hop_a)
    for i in range(1, intervals):
        for o, value in enumerate(source(i * CF)):
            ww[i, 4 + o] = state[i - 1][o] + value
    swap_w = swap(ww, 4, 2, pl.ds(1, intervals - 1))
    start(swap_w)
    received(swap0)
    received(hop_a)
    for l in range(OWN + 8):
        ww[0, l] = w0[l] + jnp.where(tm > 0, ain[l], 0.0)
    received(swap_w)

    state = all_of(ww, 4, 4)
    for _ in range(4):
        state = advance(state, fine_op)
    for o in range(OWN):
        rw0[4 + o] = state[0][o]
        rw1[3 + o] = state[1][o]
        r2[o] = state[2][o]
    swap_r0 = swap(rw0, 4, 2)
    swap_r1 = swap(rw1, 3, 2)
    start(swap_r0 + swap_r1)
    received(swap_r0)
    state = advance([read(rw0, 4, 2)], coarse_op)
    received(swap_r1)
    state = plus(state, [read(rw1, 3, 1)])
    state = advance(state, coarse_op)
    for o in range(OWN):
        lout[o] = state[0][o] + r2[o]

    hop_e = hop(eout, ein, 5, 3)

    @pl.when(tm == 0)
    def _():
        for l in range(OWN + 10):
            ein[l] = jnp.zeros((NODES, PLANE), f32)
        for o in range(OWN):
            eout[o] = lout[o]
        start(hop_e)

    @pl.when(tm > 0)
    def _():
        received(hop_e[:5])

    @pl.when(jnp.logical_and(tm > 0, tm < sections - 1))
    def _():
        state = [read(ein, 5, 3)]
        for _ in range(3):
            state = advance(state, coarse_op)
        for o in range(OWN):
            eout[o] = state[0][o] + lout[o]
        start(hop_e)

    @pl.when(tm > 0)
    def _():
        received(hop_e[5:])

    errors = [read(ein, 5, 5)]
    errors.append(plus(advance([errors[0]], coarse_op), [read(rw0, 4, 4)])[0])
    errors.append(plus(advance([errors[1]], coarse_op), [read(rw1, 3, 3)])[0])
    state = [
        [a + b for a, b in zip(read(ww, 4, 3, i), errors[i][2 - i : 2 - i + OWN + 6])]
        for i in range(intervals)
    ]

    def write(inner, state):
        for i in range(intervals):
            keep = (len(state[i]) - OWN) // 2
            for o in range(OWN):
                t = i * CF + inner
                out_ref[pl.ds(t * OWN * NODES + o, NODES, stride=OWN), :] = state[i][keep + o]

    write(0, state)
    for inner, win, halo, keep in ((1, w1, 3, 2), (2, w2, 2, 1), (3, w3, 1, 0)):
        state = plus(advance(state, fine_op), all_of(win, halo, keep))
        write(inner, state)

    for c in first_copies + hop_a + swap_w + swap_r0 + swap_r1:
        c.wait_send()

    @pl.when(tm < sections - 1)
    def _():
        for c in hop_e:
            c.wait_send()


COPIES = 16 + 5 + 4 + 4 + 4 + 7


def solution(mesh):
    sections, positions = mesh.shape["tm"], mesh.shape["space"]

    def on_device(sources, fine_volume, fine_faces, coarse_volume, coarse_faces, flow_kinds, neighbours):
        steps = sources.shape[0]
        intervals = steps // CF
        layers = OWN * positions

        def body(*refs):
            kernel(sections, positions, layers, intervals, *refs)

        def state(*lead):
            return pltpu.VMEM(lead + (NODES, PLANE), f32)

        vmem = pl.BlockSpec(memory_space=pltpu.VMEM)
        out = pl.pallas_call(
            body,
            out_shape=jax.ShapeDtypeStruct((steps * NODES * OWN, PLANE), f32),
            in_specs=[vmem] * 7,
            out_specs=vmem,
            scratch_shapes=[
                pltpu.VMEM((832, 256), bf16),
                pltpu.VMEM((832, 256), bf16),
                pltpu.VMEM((OWN + 2 * KH, 8, PLANE), f32),
                pltpu.VMEM((4, 8, PLANE), jnp.int32),
                state(OWN + 8),
                state(intervals, OWN + 6),
                state(intervals, OWN + 4),
                state(intervals, OWN + 2),
                state(OWN),
                state(OWN + 8),
                state(intervals, OWN + 8),
                state(OWN + 8),
                state(OWN + 6),
                state(OWN),
                state(OWN),
                state(OWN + 10),
                state(OWN),
                pltpu.SemaphoreType.DMA((COPIES,)),
                pltpu.SemaphoreType.DMA((COPIES,)),
            ],
            compiler_params=pltpu.CompilerParams(
                collective_id=0, has_side_effects=True, vmem_limit_bytes=56 * 1024 * 1024
            ),
        )(sources.reshape(steps * NODES * OWN, PLANE), fine_volume, fine_faces, coarse_volume, coarse_faces,
          flow_kinds, neighbours)
        return out.reshape(sources.shape)

    in_specs = (P("tm", None, "space", None), P(), P(), P(), P(), P(None, "space", None), P())
    out_specs = P("tm", None, "space", None)
    return jax.shard_map(on_device, mesh=mesh, in_specs=in_specs, out_specs=out_specs, check_vma=False)
```

time: 1390 us -> 176 us (0.13)
  the two profiles are of different devices: /device:TPU:8 before, /device:TPU:15 now
where the time goes in v1:
time: 176 us
  Pallas kernels  174 us (99%)
  local copies, waits for them, and re-layouts  2.06 us (1%)
    pallas_call x1, Pallas kernels, on_device(): pl.pallas_call(body, out_shape=jax.ShapeDtypeStruct((steps * NODES * OWN,...  174 us

profile of v1, /device:TPU:15, one launch (start us, length us, event | category | flops | bytes accessed | tf_op | source)
XLA Modules:
  0.0 175.9 jit_solution(12365115656907313993)
XLA Ops:
  0.0 173.8 %shard_map.73 = f32[1536,128]{1,0:T(8,128)} custom-call(f32[1536,128]{1,0:T(8,128)} %bitcast.3, f32[64,64]{1,0:T(8,128)} %refs_1_.1, f32[6,2,64,64]{3,2,1,0:T(8,128)} %refs_2_.1, f32[64,64]{1,0:T(8,128)} %refs_3_.1, f32[6,2,64,64]{3,2,1,0:T(8,128)} %refs_4_.1, s32[6,2,128]{2,1,0:T(2,128)} %refs_5_.1, s32[4,128]{1,0:T(4,128)} %refs_6_.1), custom_call_target="tpu_custom_call" | custom-call | tf_op jit(solution)/shard_map/pallas_call | solution.py:304
  173.8 2.1 %copy.9 = f32[12,64,2,128]{3,2,1,0:T(2,128)} copy(f32[12,64,2,128]{3,2,1,0:T(2,128)} %bitcast.2) | data formatting | bytes 1572864

commit v2 on v1

--- a/solution.py
+++ b/solution.py
@@ -9,7 +9,9 @@
 NODES = 64
 PLANE = 128
 OWN = 2
-KH = 4
+KH = 5
+HOST = 1
+LAG = 8
 MESH = pl.DeviceIdType.MESH
 f32, bf16 = jnp.float32, jnp.bfloat16
 
@@ -33,7 +35,8 @@
 def kernel(sections, positions, layers, intervals,
            x_ref, fv_ref, ff_ref, cv_ref, cf_ref, kinds_ref, nb_ref, out_ref,
            fine_op, coarse_op, kwin, idx, w0, w1, w2, w3, aout, ain, ww, rw0, rw1, r2, lout, ein, eout,
-           send_sem, recv_sem):
+           pin, pout, terms, chain,
+           send_sem, recv_sem, term_send, term_recv, home_send, home_recv, chain_send, chain_recv, token):
     tm, sp = lax.axis_index("tm"), lax.axis_index("space")
 
     def at(d, ahead):
@@ -41,9 +44,34 @@
 
     partners = [at(d, 0) for d in (-3, -2, -1, 1, 2, 3)]
     partners += [at(d, a) for a in (-1, 1) for d in range(-3, 4)]
+    partners.append((lax.rem(tm + LAG, sections), sp))
     barrier = pltpu.get_barrier_semaphore()
+    final = sections - 1
+
+    def greet(device):
+        pl.semaphore_signal(barrier, inc=1, device_id=device, device_id_type=MESH)
+
     for device in partners:
-        pl.semaphore_signal(barrier, inc=1, device_id=device, device_id_type=MESH)
+        greet(device)
+
+    @pl.when(tm == HOST)
+    def _():
+        for s in range(sections):
+            if s != HOST:
+                greet((s, sp))
+        for d in (-3, -2, -1, 1, 2, 3):
+            greet((final, at(d, 0)[1]))
+
+    @pl.when(tm != HOST)
+    def _():
+        greet((HOST, sp))
+
+    @pl.when(tm == final)
+    def _():
+        for d in (-3, -2, -1, 1, 2, 3):
+            greet((HOST, at(d, 0)[1]))
+
+    greetings = len(partners) + jnp.where(tm == HOST, sections - 1 + 6, 1) + jnp.where(tm == final, 6, 0)
 
     def source(t):
         return [x_ref[pl.ds(t * OWN * NODES + o, NODES, stride=OWN), :] for o in range(OWN)]
@@ -86,11 +114,11 @@
                 made.append(copy(win.at[lead, src], win.at[lead, dst], d, 0))
         return made
 
-    def hop(block, win, halo, reach):
+    def hop(block, win, halo, reach, ahead=1):
         made = []
         for d in [0] + [s * r for r in range(1, reach + 1) for s in (1, -1)]:
             first, size, skip = span(halo, d)
-            made.append(copy(block.at[pl.ds(skip, size)], win.at[pl.ds(first, size)], d, 1))
+            made.append(copy(block.at[pl.ds(skip, size)], win.at[pl.ds(first, size)], d, ahead))
         return made
 
     def start(copies):
@@ -103,13 +131,18 @@
 
     every = pl.ds(0, intervals)
     swap1 = swap(w1, 3, 2, every)
-    swapk = swap(kwin, KH, 2)
+    swapk = swap(kwin, KH, 3)
     swap2 = swap(w2, 2, 1, every)
     swap3 = swap(w3, 1, 1, every)
     swap0 = swap(w0, 4, 2)
     first_copies = swap1 + swapk + swap2 + swap3 + swap0
-    pl.semaphore_wait(barrier, len(partners))
-    start(first_copies)
+    pl.semaphore_wait(barrier, greetings)
+
+    @pl.when(tm >= LAG)
+    def _():
+        pl.semaphore_wait(token, 1)
+
+    start(swap1 + swapk + swap2 + swap3)
 
     rows = lax.broadcasted_iota(jnp.int32, (NODES, 2 * NODES), 0)
     cols = lax.broadcasted_iota(jnp.int32, (NODES, 2 * NODES), 1)
@@ -189,6 +222,7 @@
     received(swap1 + swapk)
     state = advance(all_of(w1, 3, 3), fine_op)
     received(swap2)
+    start(swap0)
     state = plus(state, all_of(w2, 2, 2))
     state = advance(state, fine_op)
     received(swap3)
@@ -197,17 +231,34 @@
     for o in range(OWN):
         aout[o] = state[intervals - 1][o]
     hop_a = hop(aout, ain, 4, 2)
-    start(hop_a)
+
+    @pl.when(tm < final)
+    def _():
+        start(hop_a)
+
     for i in range(1, intervals):
         for o, value in enumerate(source(i * CF)):
             ww[i, 4 + o] = state[i - 1][o] + value
     swap_w = swap(ww, 4, 2, pl.ds(1, intervals - 1))
     start(swap_w)
     received(swap0)
-    received(hop_a)
-    for l in range(OWN + 8):
-        ww[0, l] = w0[l] + jnp.where(tm > 0, ain[l], 0.0)
+
+    @pl.when(tm == 0)
+    def _():
+        for l in range(OWN + 8):
+            ww[0, l] = w0[l]
+
+    @pl.when(tm > 0)
+    def _():
+        received(hop_a)
+        for l in range(OWN + 8):
+            ww[0, l] = w0[l] + ain[l]
+
     received(swap_w)
+
+    @pl.when(tm < LAG)
+    def _():
+        pl.semaphore_signal(token, inc=1, device_id=(tm + LAG, sp), device_id_type=MESH)
 
     state = all_of(ww, 4, 4)
     for _ in range(4):
@@ -227,21 +278,119 @@
     for o in range(OWN):
         lout[o] = state[0][o] + r2[o]
 
+    even = lax.rem(tm, 2) == 0
+    hop_l = hop(lout, pin, 3, 2)
+
+    @pl.when(even)
+    def _():
+        start(hop_l)
+
+    def term(slot):
+        return pltpu.make_async_remote_copy(
+            src_ref=pout, dst_ref=terms.at[slot], send_sem=term_send, recv_sem=term_recv.at[slot],
+            device_id=(HOST, sp), device_id_type=MESH)
+
+    @pl.when(jnp.logical_not(even))
+    def _():
+        received(hop_l)
+        state = [read(pin, 3, 3)]
+        for _ in range(3):
+            state = advance(state, coarse_op)
+        for o in range(OWN):
+            pout[o] = state[0][o] + lout[o]
+
+    @pl.when(tm == final - 1)
+    def _():
+        for o in range(OWN):
+            pout[o] = lout[o]
+
+    gives = jnp.logical_or(tm == final - 1, jnp.logical_and(jnp.logical_not(even), jnp.logical_and(tm != HOST, tm < final)))
+    slot = (tm + 1) // 2 + jnp.where(even, 0, -1)
+
+    @pl.when(gives)
+    def _():
+        term(slot).start()
+
+    pairs = sections // 2
+    reaches = [s * r for r in (1, 2, 3) for s in (1, -1)]
+
+    def around(side, many=6):
+        made = []
+        for n, d in enumerate(reaches[:many]):
+            first, size, skip = span(6, d)
+            made.append(pltpu.make_async_remote_copy(
+                src_ref=chain.at[side, pl.ds(6 + skip, size)], dst_ref=chain.at[side, pl.ds(first, size)],
+                send_sem=chain_send.at[side, n], recv_sem=chain_recv.at[side, n],
+                device_id=at(d, 0), device_id_type=MESH))
+        return made
+
+    def home(side, m):
+        return pltpu.make_async_remote_copy(
+            src_ref=chain.at[side, pl.ds(6, OWN)], dst_ref=ein.at[pl.ds(5, OWN)], send_sem=home_send, recv_sem=home_recv,
+            device_id=(2 * m, sp), device_id_type=MESH)
+
+    def wait_term(m):
+        term(m).wait_recv()
+        return [terms[m, o] for o in range(OWN)]
+
+    hop_f = hop(eout, ein, 5, 3, final - HOST)
+
+    @pl.when(tm == HOST)
+    def _():
+        for o in range(OWN):
+            chain[1, 6 + o] = pout[o]
+
+        def step(m, carry):
+            side = lax.rem(m, 2)
+            copies = around(side)
+            start(copies)
+            back = home(side, m)
+            back.start()
+            received(copies)
+            state = [[chain[side, l] for l in range(OWN + 12)]]
+            for _ in range(6):
+                state = advance(state, coarse_op)
+            state = plus(state, [wait_term(m)])
+            for o in range(OWN):
+                chain[1 - side, 6 + o] = state[0][o]
+            for c in copies + [back]:
+                c.wait_send()
+            return carry
+
+        lax.fori_loop(1, pairs - 1, step, 0)
+        side = (pairs - 1) % 2
+        copies = around(side, 4)
+        start(copies)
+        back = home(side, pairs - 1)
+        back.start()
+        received(copies)
+        state = [[chain[side, l] for l in range(3, OWN + 9)]]
+        for _ in range(3):
+            state = advance(state, coarse_op)
+        state = plus(state, [wait_term(pairs - 1)])
+        for o in range(OWN):
+            eout[o] = state[0][o]
+        start(hop_f)
+        for c in copies + [back]:
+            c.wait_send()
+
+    swap_e = swap(ein, 5, 3)
     hop_e = hop(eout, ein, 5, 3)
+    receives = jnp.logical_and(even, tm > 0)
+    passes = jnp.logical_and(even, tm < final - 1)
 
     @pl.when(tm == 0)
     def _():
         for l in range(OWN + 10):
             ein[l] = jnp.zeros((NODES, PLANE), f32)
-        for o in range(OWN):
-            eout[o] = lout[o]
-        start(hop_e)
-
-    @pl.when(tm > 0)
-    def _():
-        received(hop_e[:5])
-
-    @pl.when(jnp.logical_and(tm > 0, tm < sections - 1))
+
+    @pl.when(receives)
+    def _():
+        home(0, 0).wait_recv()
+        start(swap_e)
+        received(swap_e)
+
+    @pl.when(passes)
     def _():
         state = [read(ein, 5, 3)]
         for _ in range(3):
@@ -250,9 +399,13 @@
             eout[o] = state[0][o] + lout[o]
         start(hop_e)
 
-    @pl.when(tm > 0)
-    def _():
-        received(hop_e[5:])
+    @pl.when(jnp.logical_and(jnp.logical_not(even), tm < final))
+    def _():
+        received(hop_e)
+
+    @pl.when(tm == final)
+    def _():
+        received(hop_f)
 
     errors = [read(ein, 5, 5)]
     errors.append(plus(advance([errors[0]], coarse_op), [read(rw0, 4, 4)])[0])
@@ -274,16 +427,38 @@
         state = plus(advance(state, fine_op), all_of(win, halo, keep))
         write(inner, state)
 
-    for c in first_copies + hop_a + swap_w + swap_r0 + swap_r1:
-        c.wait_send()
-
-    @pl.when(tm < sections - 1)
-    def _():
-        for c in hop_e:
+    def sent(copies):
+        for c in copies:
             c.wait_send()
 
-
-COPIES = 16 + 5 + 4 + 4 + 4 + 7
+    sent(first_copies + swap_w + swap_r0 + swap_r1)
+
+    @pl.when(tm < final)
+    def _():
+        sent(hop_a)
+
+    @pl.when(even)
+    def _():
+        sent(hop_l)
+
+    @pl.when(gives)
+    def _():
+        term(slot).wait_send()
+
+    @pl.when(receives)
+    def _():
+        sent(swap_e)
+
+    @pl.when(passes)
+    def _():
+        sent(hop_e)
+
+    @pl.when(tm == HOST)
+    def _():
+        sent(hop_f)
+
+
+COPIES = 18 + 5 + 4 + 4 + 4 + 5 + 7 + 6 + 7
 
 
 def solution(mesh):
@@ -324,8 +499,19 @@
                 state(OWN),
                 state(OWN + 10),
                 state(OWN),
+                state(OWN + 6),
+                state(OWN),
+                state(sections // 2, OWN),
+                state(2, OWN + 12),
                 pltpu.SemaphoreType.DMA((COPIES,)),
                 pltpu.SemaphoreType.DMA((COPIES,)),
+                pltpu.SemaphoreType.DMA,
+                pltpu.SemaphoreType.DMA((sections // 2,)),
+                pltpu.SemaphoreType.DMA,
+                pltpu.SemaphoreType.DMA,
+                pltpu.SemaphoreType.DMA((2, 6)),
+                pltpu.SemaphoreType.DMA((2, 6)),
+                pltpu.SemaphoreType.REGULAR,
             ],
             compiler_params=pltpu.CompilerParams(
                 collective_id=0, has_side_effects=True, vmem_limit_bytes=56 * 1024 * 1024

time: 176 us -> 145 us (0.82)
  Pallas kernels: 174 us -> 142 us
    pallas_call x1, Pallas kernels: 174 us -> 142 us  [on_device(): pl.pallas_call(body, out_shape=jax.ShapeDtypeStruct((steps * NODES * OWN,...]
where the time goes in v2:
time: 145 us
  Pallas kernels  142 us (98%)
  local copies, waits for them, and re-layouts  2.06 us (1%)
    pallas_call x1, Pallas kernels, on_device(): pl.pallas_call(body, out_shape=jax.ShapeDtypeStruct((steps * NODES * OWN,...  142 us

profile of v2, /device:TPU:15, one launch (start us, length us, event | category | flops | bytes accessed | tf_op | source)
XLA Modules:
  0.0 144.5 jit_solution(11634680436390981031)
XLA Ops:
  0.0 142.4 %shard_map.73 = f32[1536,128]{1,0:T(8,128)} custom-call(f32[1536,128]{1,0:T(8,128)} %bitcast.3, f32[64,64]{1,0:T(8,128)} %refs_1_.1, f32[6,2,64,64]{3,2,1,0:T(8,128)} %refs_2_.1, f32[64,64]{1,0:T(8,128)} %refs_3_.1, f32[6,2,64,64]{3,2,1,0:T(8,128)} %refs_4_.1, s32[6,2,128]{2,1,0:T(2,128)} %refs_5_.1, s32[4,128]{1,0:T(4,128)} %refs_6_.1), custom_call_target="tpu_custom_call" | custom-call | tf_op jit(solution)/shard_map/pallas_call | solution.py:479
  142.5 2.1 %copy.9 = f32[12,64,2,128]{3,2,1,0:T(2,128)} copy(f32[12,64,2,128]{3,2,1,0:T(2,128)} %bitcast.2) | data formatting | bytes 1572864

commit v3 on v1

--- a/solution.py
+++ b/solution.py
@@ -9,7 +9,7 @@
 NODES = 64
 PLANE = 128
 OWN = 2
-KH = 4
+KH = 5
 MESH = pl.DeviceIdType.MESH
 f32, bf16 = jnp.float32, jnp.bfloat16
 
@@ -32,28 +32,47 @@
 
 def kernel(sections, positions, layers, intervals,
            x_ref, fv_ref, ff_ref, cv_ref, cf_ref, kinds_ref, nb_ref, out_ref,
-           fine_op, coarse_op, kwin, idx, w0, w1, w2, w3, aout, ain, ww, rw0, rw1, r2, lout, ein, eout,
-           send_sem, recv_sem):
+           fine_op, coarse_op, kwin, idx, w1, w2, w3, u2, u3, aout, ain, ww, rw0, rw1, r2, lout, ein,
+           pin, pout, terms, chain,
+           send_sem, recv_sem, term_send, term_recv, home_send, home_recv, chain_send, chain_recv):
     tm, sp = lax.axis_index("tm"), lax.axis_index("space")
 
     def at(d, ahead):
         return (lax.rem(tm + ahead + sections, sections), lax.rem(sp + d + positions, positions))
 
     partners = [at(d, 0) for d in (-3, -2, -1, 1, 2, 3)]
-    partners += [at(d, a) for a in (-1, 1) for d in range(-3, 4)]
+    partners += [at(d, a) for a in (-1, 1) for d in range(-2, 3)]
     barrier = pltpu.get_barrier_semaphore()
+    final = sections - 1
+
+    def greet(device):
+        pl.semaphore_signal(barrier, inc=1, device_id=device, device_id_type=MESH)
+
     for device in partners:
-        pl.semaphore_signal(barrier, inc=1, device_id=device, device_id_type=MESH)
+        greet(device)
+
+    @pl.when(tm == final)
+    def _():
+        for s in range(final):
+            greet((s, sp))
+        for d in (-2, -1, 1, 2):
+            greet((1, at(d, 0)[1]))
+        for d in (-3, 3):
+            greet((0, at(d, 0)[1]))
+
+    @pl.when(tm < final)
+    def _():
+        greet((final, sp))
+
+    greetings = len(partners) + jnp.where(tm == final, final, 1) + jnp.where(tm == 1, 4, 0) + jnp.where(tm == 0, 2, 0)
 
     def source(t):
         return [x_ref[pl.ds(t * OWN * NODES + o, NODES, stride=OWN), :] for o in range(OWN)]
 
     for i in range(intervals):
-        for win, halo, inner in ((w1, 3, 1), (w2, 2, 2), (w3, 1, 3)):
+        for win, halo, inner in ((w1, 2, 1), (w2, 1, 2), (w3, 0, 3)):
             for o, value in enumerate(source(i * CF + inner)):
                 win[i, halo + o] = value
-    for o, value in enumerate(source(0)):
-        w0[4 + o] = value
     for f in range(4):
         idx[f] = jnp.broadcast_to(nb_ref[f : f + 1, :], (8, PLANE))
     opposite = (1, 0, 3, 2)
@@ -86,11 +105,17 @@
                 made.append(copy(win.at[lead, src], win.at[lead, dst], d, 0))
         return made
 
-    def hop(block, win, halo, reach):
+    def layer(win, halo, d, o, lead):
+        return copy(win.at[lead, pl.ds(halo + o, 1)], win.at[lead, pl.ds(halo + o - OWN * d, 1)], d, 0)
+
+    def edges(win, halo, lead):
+        return [layer(win, halo, 1, OWN - 1, lead), layer(win, halo, -1, 0, lead)]
+
+    def hop(block, win, halo, reach, ahead=1):
         made = []
         for d in [0] + [s * r for r in range(1, reach + 1) for s in (1, -1)]:
             first, size, skip = span(halo, d)
-            made.append(copy(block.at[pl.ds(skip, size)], win.at[pl.ds(first, size)], d, 1))
+            made.append(copy(block.at[pl.ds(skip, size)], win.at[pl.ds(first, size)], d, ahead))
         return made
 
     def start(copies):
@@ -102,14 +127,16 @@
             c.wait_recv()
 
     every = pl.ds(0, intervals)
-    swap1 = swap(w1, 3, 2, every)
-    swapk = swap(kwin, KH, 2)
-    swap2 = swap(w2, 2, 1, every)
-    swap3 = swap(w3, 1, 1, every)
-    swap0 = swap(w0, 4, 2)
-    first_copies = swap1 + swapk + swap2 + swap3 + swap0
-    pl.semaphore_wait(barrier, len(partners))
-    start(first_copies)
+    order = [intervals - 1] + list(range(intervals - 1))
+    edges1 = {i: edges(w1, 2, i) for i in order}
+    edges2 = {i: edges(u2, 1, i) for i in order}
+    edges3 = {i: edges(u3, 1, i) for i in order}
+    swapk = swap(kwin, KH, 3)
+    pl.semaphore_wait(barrier, greetings)
+
+    start(swapk)
+    for i in order:
+        start(edges1[i])
 
     rows = lax.broadcasted_iota(jnp.int32, (NODES, 2 * NODES), 0)
     cols = lax.broadcasted_iota(jnp.int32, (NODES, 2 * NODES), 1)
@@ -186,28 +213,54 @@
     def all_of(win, halo, keep):
         return [read(win, halo, keep, i) for i in range(intervals)]
 
-    received(swap1 + swapk)
-    state = advance(all_of(w1, 3, 3), fine_op)
-    received(swap2)
-    state = plus(state, all_of(w2, 2, 2))
-    state = advance(state, fine_op)
-    received(swap3)
-    state = plus(state, all_of(w3, 1, 1))
-    state = advance(state, fine_op)
-    for o in range(OWN):
-        aout[o] = state[intervals - 1][o]
-    hop_a = hop(aout, ain, 4, 2)
-    start(hop_a)
-    for i in range(1, intervals):
-        for o, value in enumerate(source(i * CF)):
-            ww[i, 4 + o] = state[i - 1][o] + value
+    received(swapk)
+    for i in order:
+        received(edges1[i])
+        state = plus(advance([read(w1, 2, 1, i)], fine_op), [read(w2, 1, 0, i)])[0]
+        for o in range(OWN):
+            u2[i, 1 + o] = state[o]
+        start(edges2[i])
+    for i in order:
+        received(edges2[i])
+        state = plus(advance([read(u2, 1, 1, i)], fine_op), [read(w3, 0, 0, i)])[0]
+        for o in range(OWN):
+            u3[i, 1 + o] = state[o]
+        start(edges3[i])
+    hop_a = [copy(aout, ain, 0, 1)]
+    for i in order:
+        received(edges3[i])
+        state = advance([read(u3, 1, 1, i)], fine_op)[0]
+        if i == intervals - 1:
+            for o in range(OWN):
+                aout[o] = state[o]
+
+            @pl.when(tm < final)
+            def _():
+                start(hop_a)
+        else:
+            for o, value in enumerate(source((i + 1) * CF)):
+                ww[i + 1, 4 + o] = state[o] + value
+
     swap_w = swap(ww, 4, 2, pl.ds(1, intervals - 1))
     start(swap_w)
-    received(swap0)
-    received(hop_a)
-    for l in range(OWN + 8):
-        ww[0, l] = w0[l] + jnp.where(tm > 0, ain[l], 0.0)
+
+    @pl.when(tm == 0)
+    def _():
+        for o, value in enumerate(source(0)):
+            ww[0, 4 + o] = value
+
+    @pl.when(tm > 0)
+    def _():
+        received(hop_a)
+        for o, value in enumerate(source(0)):
+            ww[0, 4 + o] = value + ain[o]
+
+    swap_w0 = swap(ww, 4, 2, 0)
+    start(swap_w0)
     received(swap_w)
+    received(swap_w0)
+    late = [layer(w1, 2, 1, 0, every), layer(w1, 2, -1, 1, every)] + edges(w2, 1, every)
+    start(late)
 
     state = all_of(ww, 4, 4)
     for _ in range(4):
@@ -216,44 +269,179 @@
         rw0[4 + o] = state[0][o]
         rw1[3 + o] = state[1][o]
         r2[o] = state[2][o]
-    swap_r0 = swap(rw0, 4, 2)
-    swap_r1 = swap(rw1, 3, 2)
-    start(swap_r0 + swap_r1)
-    received(swap_r0)
+    swap_r = swap(rw0, 4, 1) + [
+        copy(rw1.at[pl.ds(3 + o, 1)], rw1.at[pl.ds(3 + o - OWN * d, 1)], d, 0) for d, o in ((1, OWN - 1), (-1, 0))]
+    start(swap_r)
+    received(swap_r[:2])
     state = advance([read(rw0, 4, 2)], coarse_op)
-    received(swap_r1)
+    received(swap_r[2:])
     state = plus(state, [read(rw1, 3, 1)])
     state = advance(state, coarse_op)
     for o in range(OWN):
         lout[o] = state[0][o] + r2[o]
 
-    hop_e = hop(eout, ein, 5, 3)
+    rest = [copy(rw1.at[pl.ds(3 + o, 1)], rw1.at[pl.ds(3 + o - OWN * d, 1)], d, 0) for d, o in ((1, 0), (-1, 1))]
+    for win, halo in ((rw0, 4), (rw1, 3)):
+        for d in (2, -2):
+            first, size, skip = span(halo, d)
+            rest.append(copy(win.at[pl.ds(halo + skip, size)], win.at[pl.ds(first, size)], d, 0))
+
+    even = lax.rem(tm, 2) == 0
+    odd = jnp.logical_not(even)
+    hop_0 = hop(lout, chain.at[0], 6, 3, -1)
+    hop_1 = hop(lout, pin, 3, 2, -2)
+    hop_l = hop(lout, pin, 3, 2)
+    pairs_up = jnp.logical_and(odd, tm < final)
+    gives = jnp.logical_and(even, tm > 0)
+    slot = tm // 2 - jnp.where(gives, 1, 0)
+
+    def term(slot):
+        return pltpu.make_async_remote_copy(
+            src_ref=pout, dst_ref=terms.at[slot], send_sem=term_send, recv_sem=term_recv.at[slot],
+            device_id=(final, sp), device_id_type=MESH)
+
+    def sent(copies):
+        for c in copies:
+            c.wait_send()
+
+    @pl.when(tm == 0)
+    def _():
+        start(hop_0)
+        sent(hop_0)
+
+    @pl.when(tm == 1)
+    def _():
+        start(hop_1)
+        sent(hop_1)
+
+    @pl.when(pairs_up)
+    def _():
+        start(hop_l)
+        sent(hop_l)
+
+    @pl.when(tm == 2)
+    def _():
+        for o in range(OWN):
+            pout[o] = lout[o]
+        term(slot).start()
+        received(hop_l)
+
+    @pl.when(jnp.logical_and(even, tm > 2))
+    def _():
+        received(hop_l)
+        state = [read(pin, 3, 3)]
+        for _ in range(3):
+            state = advance(state, coarse_op)
+        for o in range(OWN):
+            pout[o] = state[0][o] + lout[o]
+
+        term(slot).start()
+
+    @pl.when(gives)
+    def _():
+        term(slot).wait_send()
+
+    start(rest)
+
+    pairs = sections // 2
+    reaches = [s * r for r in (3, 1, 2) for s in (1, -1)]
+
+    def around(side, skip=0):
+        made = []
+        for n, d in list(enumerate(reaches))[skip:]:
+            first, size, lead = span(6, d)
+            made.append(pltpu.make_async_remote_copy(
+                src_ref=chain.at[side, pl.ds(6 + lead, size)], dst_ref=chain.at[side, pl.ds(first, size)],
+                send_sem=chain_send.at[side, n], recv_sem=chain_recv.at[side, n],
+                device_id=at(d, 0), device_id_type=MESH))
+        return made
+
+    def home(side, m):
+        return [
+            pltpu.make_async_remote_copy(
+                src_ref=chain.at[side, pl.ds(6, OWN)], dst_ref=dst, send_sem=home_send.at[n], recv_sem=home_recv,
+                device_id=(2 * m + 1 + n, sp), device_id_type=MESH)
+            for n, dst in enumerate((ein.at[pl.ds(5, OWN)], chain.at[0, pl.ds(6, OWN)]))]
+
+    def wait_term(m):
+        term(m).wait_recv()
+        return [terms[m, o] for o in range(OWN)]
+
+    @pl.when(tm == final)
+    def _():
+        received(hop_0)
+        back = home(0, 0)
+        start(back)
+        state = [[chain[0, l] for l in range(OWN + 12)]]
+        for _ in range(3):
+            state = advance(state, coarse_op)
+        received(hop_1)
+        state = plus(state, [read(pin, 3, 3)])
+        for _ in range(3):
+            state = advance(state, coarse_op)
+        state = plus(state, [wait_term(0)])
+        for o in range(OWN):
+            chain[1, 6 + o] = state[0][o]
+        sent(back)
+
+        def step(m, carry):
+            side = lax.rem(m, 2)
+            copies = around(side)
+            start(copies)
+            back = home(side, m)
+
+            @pl.when(m == pairs - 2)
+            def _():
+                start(back[::-1])
+
+            received(copies)
+
+            @pl.when(m < pairs - 2)
+            def _():
+                start(back)
+
+            state = [[chain[side, l] for l in range(OWN + 12)]]
+            for _ in range(6):
+                state = advance(state, coarse_op)
+            state = plus(state, [wait_term(m)])
+            for o in range(OWN):
+                chain[1 - side, 6 + o] = state[0][o]
+            sent(copies + back)
+            return carry
+
+        lax.fori_loop(1, pairs - 1, step, 0)
+        for o in range(OWN):
+            ein[5 + o] = chain[(pairs - 1) % 2, 6 + o]
+
+    swap_e = swap(ein, 5, 3)
 
     @pl.when(tm == 0)
     def _():
         for l in range(OWN + 10):
             ein[l] = jnp.zeros((NODES, PLANE), f32)
-        for o in range(OWN):
-            eout[o] = lout[o]
-        start(hop_e)
-
-    @pl.when(tm > 0)
-    def _():
-        received(hop_e[:5])
-
-    @pl.when(jnp.logical_and(tm > 0, tm < sections - 1))
-    def _():
-        state = [read(ein, 5, 3)]
+
+    @pl.when(jnp.logical_and(tm > 0, tm < final))
+    def _():
+        home(0, 0)[0].wait_recv()
+
+    @pl.when(gives)
+    def _():
+        copies = around(0, 2)
+        start(copies)
+        received(copies)
+        state = [[chain[0, l] for l in range(3, OWN + 9)]]
         for _ in range(3):
             state = advance(state, coarse_op)
         for o in range(OWN):
-            eout[o] = state[0][o] + lout[o]
-        start(hop_e)
+            ein[5 + o] = state[0][o] + pin[3 + o]
+        sent(copies)
 
     @pl.when(tm > 0)
     def _():
-        received(hop_e[5:])
-
+        start(swap_e)
+        received(swap_e)
+
+    received(late + rest)
     errors = [read(ein, 5, 5)]
     errors.append(plus(advance([errors[0]], coarse_op), [read(rw0, 4, 4)])[0])
     errors.append(plus(advance([errors[1]], coarse_op), [read(rw1, 3, 3)])[0])
@@ -270,20 +458,23 @@
                 out_ref[pl.ds(t * OWN * NODES + o, NODES, stride=OWN), :] = state[i][keep + o]
 
     write(0, state)
-    for inner, win, halo, keep in ((1, w1, 3, 2), (2, w2, 2, 1), (3, w3, 1, 0)):
+    for inner, win, halo, keep in ((1, w1, 2, 2), (2, w2, 1, 1), (3, w3, 0, 0)):
         state = plus(advance(state, fine_op), all_of(win, halo, keep))
         write(inner, state)
 
-    for c in first_copies + hop_a + swap_w + swap_r0 + swap_r1:
-        c.wait_send()
-
-    @pl.when(tm < sections - 1)
-    def _():
-        for c in hop_e:
-            c.wait_send()
-
-
-COPIES = 16 + 5 + 4 + 4 + 4 + 7
+    sent([c for group in (edges1, edges2, edges3) for i in order for c in group[i]])
+    sent(swapk + swap_w + swap_w0 + swap_r + late + rest)
+
+    @pl.when(tm < final)
+    def _():
+        sent(hop_a)
+
+    @pl.when(tm > 0)
+    def _():
+        sent(swap_e)
+
+
+COPIES = 18 + 6 + 1 + 4 + 4 + 4 + 4 + 6 + 7 + 5 + 5 + 6
 
 
 def solution(mesh):
@@ -311,21 +502,31 @@
                 pltpu.VMEM((832, 256), bf16),
                 pltpu.VMEM((OWN + 2 * KH, 8, PLANE), f32),
                 pltpu.VMEM((4, 8, PLANE), jnp.int32),
-                state(OWN + 8),
-                state(intervals, OWN + 6),
                 state(intervals, OWN + 4),
                 state(intervals, OWN + 2),
+                state(intervals, OWN),
+                state(intervals, OWN + 2),
+                state(intervals, OWN + 2),
                 state(OWN),
-                state(OWN + 8),
+                state(OWN),
                 state(intervals, OWN + 8),
                 state(OWN + 8),
                 state(OWN + 6),
                 state(OWN),
                 state(OWN),
                 state(OWN + 10),
+                state(OWN + 6),
                 state(OWN),
+                state(sections // 2, OWN),
+                state(2, OWN + 12),
                 pltpu.SemaphoreType.DMA((COPIES,)),
                 pltpu.SemaphoreType.DMA((COPIES,)),
+                pltpu.SemaphoreType.DMA,
+                pltpu.SemaphoreType.DMA((sections // 2,)),
+                pltpu.SemaphoreType.DMA((2,)),
+                pltpu.SemaphoreType.DMA,
+                pltpu.SemaphoreType.DMA((2, 6)),
+                pltpu.SemaphoreType.DMA((2, 6)),
             ],
             compiler_params=pltpu.CompilerParams(
                 collective_id=0, has_side_effects=True, vmem_limit_bytes=56 * 1024 * 1024

time: 176 us -> 134 us (0.76)
  Pallas kernels: 174 us -> 132 us
    pallas_call x1, Pallas kernels: 174 us -> 132 us  [on_device(): pl.pallas_call(body, out_shape=jax.ShapeDtypeStruct((steps * NODES * OWN,...]
where the time goes in v3:
time: 134 us
  Pallas kernels  132 us (99%)
  local copies, waits for them, and re-layouts  2.06 us (2%)
    pallas_call x1, Pallas kernels, on_device(): pl.pallas_call(body, out_shape=jax.ShapeDtypeStruct((steps * NODES * OWN,...  132 us

profile of v3, /device:TPU:15, one launch (start us, length us, event | category | flops | bytes accessed | tf_op | source)
XLA Modules:
  0.0 133.9 jit_solution(6459256960089077790)
XLA Ops:
  0.0 131.8 %shard_map.73 = f32[1536,128]{1,0:T(8,128)} custom-call(f32[1536,128]{1,0:T(8,128)} %bitcast.3, f32[64,64]{1,0:T(8,128)} %refs_1_.1, f32[6,2,64,64]{3,2,1,0:T(8,128)} %refs_2_.1, f32[64,64]{1,0:T(8,128)} %refs_3_.1, f32[6,2,64,64]{3,2,1,0:T(8,128)} %refs_4_.1, s32[6,2,128]{2,1,0:T(2,128)} %refs_5_.1, s32[4,128]{1,0:T(4,128)} %refs_6_.1), custom_call_target="tpu_custom_call" | custom-call | tf_op jit(solution)/shard_map/pallas_call | solution.py:495
  131.8 2.1 %copy.9 = f32[12,64,2,128]{3,2,1,0:T(2,128)} copy(f32[12,64,2,128]{3,2,1,0:T(2,128)} %bitcast.2) | data formatting | bytes 1572864

commit v4 on v3

--- a/solution.py
+++ b/solution.py
@@ -96,7 +96,7 @@
 
     def swap(win, halo, reach, lead=None):
         made = []
-        for d in [s * r for r in range(1, reach + 1) for s in (1, -1)]:
+        for d in [s * r for r in (3, 1, 2) if r <= reach for s in (1, -1)]:
             first, size, skip = span(halo, d)
             src, dst = pl.ds(halo + skip, size), pl.ds(first, size)
             if lead is None:
@@ -134,9 +134,9 @@
     swapk = swap(kwin, KH, 3)
     pl.semaphore_wait(barrier, greetings)
 
-    start(swapk)
     for i in order:
         start(edges1[i])
+    start(swapk)
 
     rows = lax.broadcasted_iota(jnp.int32, (NODES, 2 * NODES), 0)
     cols = lax.broadcasted_iota(jnp.int32, (NODES, 2 * NODES), 1)
@@ -157,8 +157,9 @@
 
     def clean(values):
         halo = (len(values) - OWN) // 2
+        edge = set(range(halo - 1, -1, -OWN)) | set(range(halo + OWN, len(values), OWN))
         return [
-            v if halo <= l < halo + OWN else jnp.where(inside(sp * OWN - halo + l), v, 0.0)
+            jnp.where(inside(sp * OWN - halo + l), v, 0.0) if l in edge else v
             for l, v in enumerate(values)
         ]
 
@@ -213,7 +214,6 @@
     def all_of(win, halo, keep):
         return [read(win, halo, keep, i) for i in range(intervals)]
 
-    received(swapk)
     for i in order:
         received(edges1[i])
         state = plus(advance([read(w1, 2, 1, i)], fine_op), [read(w2, 1, 0, i)])[0]
@@ -259,6 +259,7 @@
     start(swap_w0)
     received(swap_w)
     received(swap_w0)
+    received(swapk)
     late = [layer(w1, 2, 1, 0, every), layer(w1, 2, -1, 1, every)] + edges(w2, 1, every)
     start(late)
 
@@ -382,13 +383,16 @@
         state = plus(state, [wait_term(0)])
         for o in range(OWN):
             chain[1, 6 + o] = state[0][o]
-        sent(back)
-
         def step(m, carry):
             side = lax.rem(m, 2)
             copies = around(side)
             start(copies)
             back = home(side, m)
+            sent(home(1 - side, m - 1))
+
+            @pl.when(m > 1)
+            def _():
+                sent(around(1 - side))
 
             @pl.when(m == pairs - 2)
             def _():
@@ -406,7 +410,6 @@
             state = plus(state, [wait_term(m)])
             for o in range(OWN):
                 chain[1 - side, 6 + o] = state[0][o]
-            sent(copies + back)
             return carry
 
         lax.fori_loop(1, pairs - 1, step, 0)
@@ -463,6 +466,11 @@
         write(inner, state)
 
     sent([c for group in (edges1, edges2, edges3) for i in order for c in group[i]])
+    @pl.when(tm == final)
+    def _():
+        last = (pairs - 2) % 2
+        sent(around(last) + home(last, pairs - 2))
+
     sent(swapk + swap_w + swap_w0 + swap_r + late + rest)
 
     @pl.when(tm < final)

time: 134 us -> 132 us (0.985)
  Pallas kernels: 132 us -> 129 us
    pallas_call x1, Pallas kernels: 132 us -> 129 us  [on_device(): pl.pallas_call(body, out_shape=jax.ShapeDtypeStruct((steps * NODES * OWN,...]
where the time goes in v4:
time: 132 us
  Pallas kernels  129 us (98%)
  local copies, waits for them, and re-layouts  2.06 us (2%)
    pallas_call x1, Pallas kernels, on_device(): pl.pallas_call(body, out_shape=jax.ShapeDtypeStruct((steps * NODES * OWN,...  129 us

profile of v4, /device:TPU:15, one launch (start us, length us, event | category | flops | bytes accessed | tf_op | source)
XLA Modules:
  0.0 131.6 jit_solution(1518816662833306699)
XLA Ops:
  0.0 129.5 %shard_map.73 = f32[1536,128]{1,0:T(8,128)} custom-call(f32[1536,128]{1,0:T(8,128)} %bitcast.3, f32[64,64]{1,0:T(8,128)} %refs_1_.1, f32[6,2,64,64]{3,2,1,0:T(8,128)} %refs_2_.1, f32[64,64]{1,0:T(8,128)} %refs_3_.1, f32[6,2,64,64]{3,2,1,0:T(8,128)} %refs_4_.1, s32[6,2,128]{2,1,0:T(2,128)} %refs_5_.1, s32[4,128]{1,0:T(4,128)} %refs_6_.1), custom_call_target="tpu_custom_call" | custom-call | tf_op jit(solution)/shard_map/pallas_call | solution.py:503
  129.5 2.1 %copy.9 = f32[12,64,2,128]{3,2,1,0:T(2,128)} copy(f32[12,64,2,128]{3,2,1,0:T(2,128)} %bitcast.2) | data formatting | bytes 1572864

commit v5 on v4

--- a/solution.py
+++ b/solution.py
@@ -261,7 +261,11 @@
     received(swap_w0)
     received(swapk)
     late = [layer(w1, 2, 1, 0, every), layer(w1, 2, -1, 1, every)] + edges(w2, 1, every)
-    start(late)
+
+    @pl.when(tm >= sections - 2)
+    def _():
+        start(late)
+
 
     state = all_of(ww, 4, 4)
     for _ in range(4):
@@ -343,6 +347,10 @@
         term(slot).wait_send()
 
     start(rest)
+
+    @pl.when(tm < sections - 2)
+    def _():
+        start(late)
 
     pairs = sections // 2
     reaches = [s * r for r in (3, 1, 2) for s in (1, -1)]

time: 132 us -> 130 us (0.985)
    pallas_call x1, Pallas kernels: 129 us -> 128 us  [on_device(): pl.pallas_call(body, out_shape=jax.ShapeDtypeStruct((steps * NODES * OWN,...]
where the time goes in v5:
time: 130 us
  Pallas kernels  128 us (98%)
  local copies, waits for them, and re-layouts  2.06 us (2%)
    pallas_call x1, Pallas kernels, on_device(): pl.pallas_call(body, out_shape=jax.ShapeDtypeStruct((steps * NODES * OWN,...  128 us

profile of v5, /device:TPU:15, one launch (start us, length us, event | category | flops | bytes accessed | tf_op | source)
XLA Modules:
  0.0 130.2 jit_solution(16874752087195598540)
XLA Ops:
  0.0 128.1 %shard_map.73 = f32[1536,128]{1,0:T(8,128)} custom-call(f32[1536,128]{1,0:T(8,128)} %bitcast.3, f32[64,64]{1,0:T(8,128)} %refs_1_.1, f32[6,2,64,64]{3,2,1,0:T(8,128)} %refs_2_.1, f32[64,64]{1,0:T(8,128)} %refs_3_.1, f32[6,2,64,64]{3,2,1,0:T(8,128)} %refs_4_.1, s32[6,2,128]{2,1,0:T(2,128)} %refs_5_.1, s32[4,128]{1,0:T(4,128)} %refs_6_.1), custom_call_target="tpu_custom_call" | custom-call | tf_op jit(solution)/shard_map/pallas_call | solution.py:511
  128.2 2.1 %copy.9 = f32[12,64,2,128]{3,2,1,0:T(2,128)} copy(f32[12,64,2,128]{3,2,1,0:T(2,128)} %bitcast.2) | data formatting | bytes 1572864
